TPU v7x, 256 devices: a whole 4x4x8 slice. The times are simulated.
256 devices in a mesh: band: 4 (over z_hi, core), sx: 4 (over x), sy: 16 (over y, z_lo).
Axes of the slice: x: 4, y: 4, z: 8 (z_hi: 2, z_lo: 4; z = z_hi * 4 + z_lo), core: 2. Of those that a mesh axis runs over, the one named last changes fastest.
Arguments:
- orbitals: float32 [256, 24, 96, 128], P('band', 'sx', 'sy'), may hold values from -6 to 6
- potential: float32 [24, 96, 128], P('sx', 'sy'), may hold values from -3 to 0
- projectors: float32 [256, 4, 5, 128], P(('sx', 'sy')), may hold values from -0.25 to 0.25
- energies: float32 [256, 4], P(('sx', 'sy')), may hold values from 1 to 6
- centers: int32 [256, 2], P(('sx', 'sy')), may hold values from 0 to 95, as said below
Outputs:
- filtered: float32 [256, 24, 96, 128], P('band', 'sx', 'sy')
- gram: float32 [256, 256], P('band')
Inputs may be any that keep to these rules, and one draw needn't show every extreme that they name: `centers`: atom a's cell lies in the grid slab of the device numbered a // 4 along sx+sy, sy counting fastest; the first entry indexes the first grid dimension, the second the second.
All inputs are finite; a program needn't handle non-finite values.
Results may differ from a plain program's by a relative error of at most 0.0022.
Values may be sent and summed in bfloat16 or wider, within the bound.
A program may use at most 64 MiB of HBM per device.

v0:
```python
import jax
import jax.numpy as jnp
from jax import lax
from jax.sharding import PartitionSpec as P

stencil_weights = (
    -5369.0 / 1800.0,
    12.0 / 7.0,
    -15.0 / 56.0,
    10.0 / 189.0,
    -1.0 / 112.0,
    2.0 / 1925.0,
    -1.0 / 16632.0,
)
filter_center = 6.5
filter_half = 6.0
offsets_x = (0, -1, 1, 0, 0)
offsets_y = (0, 0, 0, -1, 1)


def from_behind(block, axis, distance):
    devices = range(lax.axis_size(axis))
    route = [(i - distance, i) for i in devices if i - distance in devices]
    return lax.ppermute(block, axis, route)


def extended(cells, sides, width):
    for axis, dim in sides:
        count = lax.axis_size(axis)
        ends = count - 1
        head = lax.slice_in_dim(cells, 0, width, axis=dim)
        tail = lax.slice_in_dim(cells, cells.shape[dim] - width, cells.shape[dim], axis=dim)
        cells = jnp.concatenate(
            [
                lax.ppermute(tail, axis, [(i, (i + 1) % count) for i in range(ends)]),
                cells,
                lax.ppermute(head, axis, [((i + 1) % count, i) for i in range(ends)]),
            ],
            axis=dim,
        )
    return cells


def second_sum(ext_x, ext_y, field):
    count_x = field.shape[1]
    count_y = field.shape[2]
    count_z = field.shape[3]
    padded_z = jnp.pad(field, ((0, 0), (0, 0), (0, 0), (6, 6)))
    total = 3.0 * stencil_weights[0] * field
    for step in range(1, 7):
        weight = stencil_weights[step]
        total = total + weight * (
            ext_x[:, 6 + step : 6 + step + count_x] + ext_x[:, 6 - step : 6 - step + count_x]
        )
        total = total + weight * (
            ext_y[:, :, 6 + step : 6 + step + count_y] + ext_y[:, :, 6 - step : 6 - step + count_y]
        )
        total = total + weight * (
            padded_z[:, :, :, 6 + step : 6 + step + count_z]
            + padded_z[:, :, :, 6 - step : 6 - step + count_z]
        )
    return total


def column_slots(centers, first_x, first_y, count_x, count_y):
    shift_x = jnp.array(offsets_x, jnp.int32)
    shift_y = jnp.array(offsets_y, jnp.int32)
    local_x = centers[:, 0:1] - first_x + shift_x[None, :]
    local_y = centers[:, 1:2] - first_y + shift_y[None, :]
    inner = count_x * count_y
    slots = jnp.where(
        local_x < 0,
        inner + local_y,
        jnp.where(
            local_x >= count_x,
            inner + count_y + local_y,
            jnp.where(
                local_y < 0,
                inner + 2 * count_y + local_x,
                jnp.where(
                    local_y >= count_y,
                    inner + 2 * count_y + count_x + local_x,
                    local_x * count_y + local_y,
                ),
            ),
        ),
    )
    return slots.reshape(-1)


def pass_x(strip, offset):
    return from_behind(strip.astype(jnp.bfloat16), "sx", offset).astype(strip.dtype)


def pass_y(strip, offset):
    return from_behind(strip, "sy", offset)


def nonlocal_term(field, ext_x, ext_y, slots, projectors, energies):
    batch, count_x, count_y, count_z = field.shape
    inner = count_x * count_y
    tiles = projectors.shape[2]
    atoms = projectors.shape[0]
    table = jnp.concatenate(
        [
            field.reshape(batch, inner, count_z),
            ext_x[:, 5],
            ext_x[:, 6 + count_x],
            ext_y[:, :, 5],
            ext_y[:, :, 6 + count_y],
        ],
        axis=1,
    )
    onehot = (slots[:, None] == jnp.arange(table.shape[1], dtype=jnp.int32)[None, :]).astype(
        jnp.float32
    )
    picked = jnp.einsum("kc,bcz->bkz", onehot, table, precision=lax.Precision.HIGHEST).reshape(
        batch, atoms, tiles, count_z
    )
    coeffs = jnp.einsum("aptz,batz->bap", projectors, picked, precision=lax.Precision.HIGHEST)
    weighted = coeffs * energies[None]
    spread = jnp.einsum(
        "aptz,bap->batz", projectors, weighted, precision=lax.Precision.HIGHEST
    ).reshape(batch, atoms * tiles, count_z)
    back = jnp.einsum("kc,bkz->bcz", onehot, spread, precision=lax.Precision.HIGHEST)
    result = back[:, :inner].reshape(batch, count_x, count_y, count_z)
    from_right = pass_x(back[:, inner : inner + count_y], -1)
    from_left = pass_x(back[:, inner + count_y : inner + 2 * count_y], 1)
    result = result.at[:, count_x - 1].add(from_right)
    result = result.at[:, 0].add(from_left)
    base_y = inner + 2 * count_y
    from_above = pass_y(back[:, base_y : base_y + count_x], -1)
    from_below = pass_y(back[:, base_y + count_x : base_y + 2 * count_x], 1)
    result = result.at[:, :, count_y - 1].add(from_above)
    result = result.at[:, :, 0].add(from_below)
    return result


def local(orbitals, potential, projectors, energies, centers):
    first_y = lax.axis_index("sy") * potential.shape[1]
    pot_all, proj_all, energy_all = (potential, projectors, energies)
    slots = column_slots(
        centers,
        lax.axis_index("sx") * potential.shape[0],
        first_y,
        orbitals.shape[1],
        orbitals.shape[2],
    )

    def apply_h(vector):
        ext_x = extended(vector, (("sx", 1),), 6)
        ext_y = extended(vector, (("sy", 2),), 6)
        kinetic = -0.5 * second_sum(ext_x, ext_y, vector)
        return (
            kinetic
            + pot_all[None] * vector
            + nonlocal_term(vector, ext_x, ext_y, slots, proj_all, energy_all)
        )

    previous = orbitals
    current = (apply_h(orbitals) - filter_center * orbitals) / filter_half
    following = 2.0 * (apply_h(current) - filter_center * current) / filter_half - previous
    previous, current = (current, following)
    rounded = current.astype(jnp.bfloat16)
    flat = rounded.reshape(rounded.shape[0], -1)
    partial_rows = lax.dot_general(
        flat,
        lax.all_gather(flat, "band", axis=0, tiled=True),
        (((1,), (1,)), ((), ())),
        preferred_element_type=jnp.float32,
    )
    cell_total = flat.shape[1] * lax.axis_size("sx") * lax.axis_size("sy")
    gram = lax.psum(partial_rows, ("sx", "sy")) / cell_total
    return (current, gram)


def solution(mesh):
    in_specs = (
        P("band", "sx", "sy", None),
        P("sx", "sy", None),
        P(("sx", "sy"), None, None, None),
        P(("sx", "sy"), None),
        P(("sx", "sy"), None),
    )
    out_specs = (P("band", "sx", "sy", None), P("band", None))
    return jax.shard_map(local, mesh=mesh, in_specs=in_specs, out_specs=out_specs, check_vma=False)
```

profile of v0, /device:TPU:128, one launch (start us, length us, event | category | flops | bytes accessed | tf_op | source)
XLA Modules:
  0.0 955.3 jit_solution(861587233101737842)
XLA Ops:
  8.6 4.6 collective-permute-start.1
  13.2 4.0 collective-permute-start.3
  18.5 3.1 copy.96
  21.8 15.3 %collective-permute-done = f32[64,6,6,128]{3,0,2,1:T(8,128)S(1)} collective-permute-done((f32[64,6,6,128]{3,0,2,1:T(8,128)}, f32[64,6,6,128]{3,0,2,1:T(8,128)S(1)}, u32[]{:S(2)}, u32[]{:S(2)}) %collective-permute-start) | collective-permute-done | bytes 1179680 | tf_op jit(solution)/shard_map/ppermute | solution.py:37
  41.1 2.0 copy_dynamic-update-slice_fusion.2
  43.1 2.5 copy_dynamic-update-slice_fusion
  45.6 25.1 %collective-permute-done.2 = f32[64,6,6,128]{3,0,2,1:T(8,128)} collective-permute-done((f32[64,6,6,128]{3,0,2,1:T(8,128)}, f32[64,6,6,128]{3,0,2,1:T(8,128)}, u32[]{:S(2)}, u32[]{:S(2)}) %collective-permute-start.2) | collective-permute-done | bytes 1179680 | tf_op jit(solution)/shard_map/ppermute | solution.py:37
  70.7 3.1 copy_dynamic-update-slice_fusion.3
  74.7 14.2 %concatenate.86 = f32[64,60,128]{2,1,0:T(8,128)} concatenate(f32[64,36,128]{2,1,0:T(8,128)} %copy.96, f32[64,6,128]{2,1,0:T(8,128)} %bitcast.115, f32[64,6,128]{2,1,0:T(8,128)S(1)} %bitcast.114, f32[64,6,128]{2,1,0:T(8,128)} %get-tuple-element.126, f32[64,6,128]{2,1,0:T(8,128)} %get-tuple-element.125), dimensions={1} | concatenate | bytes 3932160 | tf_op jit(solution)/shard_map/concatenate | solution.py:104
  88.9 2.5 convolution_bitcast_fusion.3
  98.2 4.7 collective-permute-start.5
  104.2 5.3 collective-permute-start.7
  109.4 1.9 copy.78
  111.4 1.8 copy.79
  113.2 1.8 copy.102
  115.3 6.1 scatter-add.29
  124.9 34.7 %broadcast_multiply_fusion = (f32[64,6,6,128]{3,1,0,2:T(8,128)S(1)}, f32[64,6,6,128]{3,1,0,2:T(8,128)}) fusion(f32[64,6,6,128]{3,1,0,2:T(8,128)} %get-tuple-element.116, f32[64,6,6,128]{3,1,0,2:T(8,128)} %fusion.135, f32[6,6,128]{2,0,1:T(8,128)S(1)} %copy.90, f32[64,6,6,128]{3,0,2,1:T(8,128)} %collective-permute-done.3, ...), kind=kLoop, calls=%fused_computation.225 | loop fusion | flops 21233664 | bytes 21252096 | tf_op jit(solution)/shard_map/div | solution.py:161
  162.5 4.6 collective-permute-start.11
  167.1 4.8 collective-permute-start.9
  172.7 15.8 %collective-permute-done.8 = f32[64,6,6,128]{3,0,2,1:T(8,128)S(1)} collective-permute-done((f32[64,6,6,128]{3,0,2,1:T(8,128)S(1)}, f32[64,6,6,128]{3,0,2,1:T(8,128)S(1)}, u32[]{:S(2)}, u32[]{:S(2)}) %collective-permute-start.8) | collective-permute-done | bytes 1179680 | tf_op jit(solution)/shard_map/ppermute | solution.py:37
  189.6 2.6 collective-permute-done.10
  196.3 6.5 concatenate.91
  210.5 5.3 collective-permute-start.13
  217.2 4.8 collective-permute-start.15
  222.0 1.9 copy.105
  223.9 1.9 copy.107
  225.9 1.8 copy.128
  227.9 6.2 scatter-add.35
  237.5 15.2 %fusion.152 = (bf16[64,6,6,128]{3,1,0,2:T(8,128)(2,1)S(1)}, f32[64,6,6,128]{3,1,0,2:T(8,128)}) fusion(f32[64,6,6,128]{3,0,2,1:T(8,128)S(1)} %copy-done.4, f32[64,6,6,128]{3,1,0,2:T(8,128)} %get-tuple-element.107, f32[64,6,6,128]{3,1,0,2:T(8,128)} %fusion.133, f32[6,6,128]{2,0,1:T(8,128)S(1)} %copy.116, f32[64,6,6,128]{3,1,0,2:T(8,128)} %copy-done.5, ...), kind=kLoop, calls=%fused_computation.274 | loop fusion | flops 24772608 | bytes 11225088 | tf_op jit(solution)/shard_map/convert_element_type | solution.py:164
  255.0 65.0 %all-gather.2.cloned.1.call-done = bf16[256,4608]{1,0:T(8,128)(2,1)} async-done(((bf16[64,4608]{1,0:T(8,128)(2,1)}), bf16[256,4608]{1,0:T(8,128)(2,1)}) %all-gather.2.cloned.1.call-update) | async-done | bytes 2359312 | tf_op jit(solution)/shard_map/all_gather | solution.py:168
  320.0 3.3 fusion.160
  324.6 622.4 %all-reduce.4.cloned.1.call-done = f32[64,256]{1,0:T(8,128)} async-done(((f32[64,256]{1,0:T(8,128)}), f32[64,256]{1,0:T(8,128)}) %all-reduce.4.cloned.1.call-update) | async-done | bytes 65552 | tf_op jit(solution)/shard_map/psum | solution.py:173
  (122 shorter events, 45.8 us)
Async XLA Ops:
  7.2 84.3 %copy-start = (f32[4,4,5,128]{3,1,2,0:T(4,128)S(1)}, f32[4,4,5,128]{3,1,2,0:T(4,128)}, u32[]{:S(2)}) copy-start(f32[4,4,5,128]{3,1,2,0:T(4,128)} %param.25) | copy-start | bytes 122884
  7.2 14.5 %copy-start.19 = (s32[5]{0:T(128)S(1)}, s32[5]{0:T(128)}, u32[]{:S(2)}) copy-start(s32[5]{0:T(128)} %constant.246.clone) | copy-start | bytes 64
  7.2 14.5 %copy-start.20 = (s32[5]{0:T(128)S(1)}, s32[5]{0:T(128)}, u32[]{:S(2)}) copy-start(s32[5]{0:T(128)} %constant.247.clone) | copy-start | bytes 64
  7.2 14.4 %copy-start.18 = (s32[4,2]{0,1:T(2,128)S(1)}, s32[4,2]{0,1:T(2,128)}, u32[]{:S(2)}) copy-start(s32[4,2]{0,1:T(2,128)} %param.27) | copy-start | bytes 100
  7.2 14.6 %copy-start.16 = (f32[6,6,128]{2,1,0:T(8,128)S(1)}, f32[6,6,128]{2,1,0:T(8,128)}, u32[]{:S(2)}) copy-start(f32[6,6,128]{2,1,0:T(8,128)} %param.24) | copy-start | bytes 55300
  7.2 312.8 %all-gather.2.cloned.1.call-start = ((), (), s32[]{:S(2)}) async-start(), calls=%async_computation | async-start | bytes 2949120 | tf_op jit(solution)/shard_map/all_gather | solution.py:168
  7.3 29.8 %collective-permute-start = (f32[64,6,6,128]{3,0,2,1:T(8,128)}, f32[64,6,6,128]{3,0,2,1:T(8,128)S(1)}, u32[]{:S(2)}, u32[]{:S(2)}) collective-permute-start(f32[64,6,6,128]{3,0,2,1:T(8,128)} %param.23), channel_id=1, source_target_pairs={{16,0},{32,16},{48,32},{17,1},{33,17},{49,33},{18,2},{34,18},{50,3... | collective-permute-start | bytes 3538952 | tf_op jit(solution)/shard_map/ppermute | solution.py:37
  8.6 29.8 %collective-permute-start.1 = (f32[64,6,6,128]{3,0,2,1:T(8,128)}, f32[64,6,6,128]{3,0,2,1:T(8,128)S(1)}, u32[]{:S(2)}, u32[]{:S(2)}) collective-permute-start(f32[64,6,6,128]{3,0,2,1:T(8,128)} %param.23), channel_id=1, source_target_pairs={{0,16},{16,32},{32,48},{1,17},{17,33},{33,49},{2,18},{18,34},{34,5... | collective-permute-start | bytes 3538952 | tf_op jit(solution)/shard_map/ppermute | solution.py:35
  13.2 27.9 %collective-permute-start.3 = (f32[64,6,6,128]{3,0,2,1:T(8,128)}, f32[64,6,6,128]{3,0,2,1:T(8,128)}, u32[]{:S(2)}, u32[]{:S(2)}) collective-permute-start(f32[64,6,6,128]{3,0,2,1:T(8,128)} %param.23), channel_id=1, source_target_pairs={{0,1},{1,2},{2,3},{3,4},{4,5},{5,6},{6,7},{7,8},{8,9},{9,10},{10,1... | collective-permute-start | bytes 3538952 | tf_op jit(solution)/shard_map/ppermute | solution.py:35
  17.2 53.5 %collective-permute-start.2 = (f32[64,6,6,128]{3,0,2,1:T(8,128)}, f32[64,6,6,128]{3,0,2,1:T(8,128)}, u32[]{:S(2)}, u32[]{:S(2)}) collective-permute-start(f32[64,6,6,128]{3,0,2,1:T(8,128)} %param.23), channel_id=1, source_target_pairs={{1,0},{2,1},{3,2},{4,3},{5,4},{6,5},{7,6},{8,7},{9,8},{10,9},{11,1... | collective-permute-start | bytes 3538952 | tf_op jit(solution)/shard_map/ppermute | solution.py:37
  39.5 3.6 copy-start.3
  95.7 17.5 %collective-permute-start.4 = (bf16[64,6,128]{2,0,1:T(8,128)(2,1)S(1)}, bf16[64,6,128]{2,0,1:T(8,128)(2,1)S(1)}, u32[]{:S(2)}, u32[]{:S(2)}) collective-permute-start(bf16[64,6,128]{2,0,1:T(8,128)(2,1)S(1)} %get-tuple-element.122), channel_id=1, source_target_pairs={{16,0},{32,16},{48,32},{17,1},{33,17},{49,33},{18,2},{34,18},{50,3... | collective-permute-start | bytes 294920 | tf_op jit(solution)/shard_map/ppermute | solution.py:24
  97.9 11.5 %copy-start.9 = (f32[64,6,6,128]{3,0,2,1:T(8,128)S(1)}, f32[64,6,6,128]{3,0,2,1:T(8,128)}, u32[]{:S(2)}) copy-start(f32[64,6,6,128]{3,0,2,1:T(8,128)} %copy-done.8) | copy-start | bytes 3538948
  98.2 13.2 %copy-start.11 = (f32[64,6,6,128]{3,0,2,1:T(8,128)S(1)}, f32[64,6,6,128]{3,0,2,1:T(8,128)}, u32[]{:S(2)}) copy-start(f32[64,6,6,128]{3,0,2,1:T(8,128)} %copy-done.10) | copy-start | bytes 3538948
  98.2 16.9 %collective-permute-start.5 = (bf16[64,6,128]{2,0,1:T(8,128)(2,1)S(1)}, bf16[64,6,128]{2,0,1:T(8,128)(2,1)S(1)}, u32[]{:S(2)}, u32[]{:S(2)}) collective-permute-start(bf16[64,6,128]{2,0,1:T(8,128)(2,1)S(1)} %get-tuple-element.121), channel_id=1, source_target_pairs={{0,16},{16,32},{32,48},{1,17},{17,33},{33,49},{2,18},{18,34},{34,5... | collective-permute-start | bytes 294920 | tf_op jit(solution)/shard_map/ppermute | solution.py:24
  102.9 18.5 %collective-permute-start.6 = (f32[64,6,128]{2,1,0:T(8,128)}, f32[64,6,128]{2,1,0:T(8,128)}, u32[]{:S(2)}, u32[]{:S(2)}) collective-permute-start(f32[64,6,128]{2,1,0:T(8,128)} %get-tuple-element.111), channel_id=1, source_target_pairs={{1,0},{2,1},{3,2},{4,3},{5,4},{6,5},{7,6},{8,7},{9,8},{10,9},{11,1... | collective-permute-start | bytes 589832 | tf_op jit(solution)/shard_map/ppermute | solution.py:24
  104.2 19.0 %collective-permute-start.7 = (f32[64,6,128]{2,1,0:T(8,128)}, f32[64,6,128]{2,1,0:T(8,128)}, u32[]{:S(2)}, u32[]{:S(2)}) collective-permute-start(f32[64,6,128]{2,1,0:T(8,128)} %get-tuple-element.110), channel_id=1, source_target_pairs={{0,1},{1,2},{2,3},{3,4},{4,5},{5,6},{6,7},{7,8},{8,9},{9,10},{10,1... | collective-permute-start | bytes 589832 | tf_op jit(solution)/shard_map/ppermute | solution.py:24
  159.6 13.1 %copy-start.1 = (f32[64,6,6,128]{3,1,0,2:T(8,128)}, f32[64,6,6,128]{3,1,0,2:T(8,128)S(1)}, u32[]{:S(2)}) copy-start(f32[64,6,6,128]{3,1,0,2:T(8,128)S(1)} %get-tuple-element.106) | copy-start | bytes 3538948
  159.9 28.7 %collective-permute-start.8 = (f32[64,6,6,128]{3,0,2,1:T(8,128)S(1)}, f32[64,6,6,128]{3,0,2,1:T(8,128)S(1)}, u32[]{:S(2)}, u32[]{:S(2)}) collective-permute-start(f32[64,6,6,128]{3,0,2,1:T(8,128)S(1)} %copy.104), channel_id=1, source_target_pairs={{16,0},{32,16},{48,32},{17,1},{33,17},{49,33},{18,2},{34,18},{50,3... | collective-permute-start | bytes 3538952 | tf_op jit(solution)/shard_map/ppermute | solution.py:37
  161.2 31.0 %collective-permute-start.10 = (f32[64,6,6,128]{3,0,2,1:T(8,128)S(1)}, f32[64,6,6,128]{3,0,2,1:T(8,128)S(1)}, u32[]{:S(2)}, u32[]{:S(2)}) collective-permute-start(f32[64,6,6,128]{3,0,2,1:T(8,128)S(1)} %copy.104), channel_id=1, source_target_pairs={{1,0},{2,1},{3,2},{4,3},{5,4},{6,5},{7,6},{8,7},{9,8},{10,9},{11,1... | collective-permute-start | bytes 3538952 | tf_op jit(solution)/shard_map/ppermute | solution.py:37
  162.5 30.4 %collective-permute-start.11 = (f32[64,6,6,128]{3,0,2,1:T(8,128)S(1)}, f32[64,6,6,128]{3,0,2,1:T(8,128)S(1)}, u32[]{:S(2)}, u32[]{:S(2)}) collective-permute-start(f32[64,6,6,128]{3,0,2,1:T(8,128)S(1)} %copy.104), channel_id=1, source_target_pairs={{0,1},{1,2},{2,3},{3,4},{4,5},{5,6},{6,7},{7,8},{8,9},{9,10},{10,1... | collective-permute-start | bytes 3538952 | tf_op jit(solution)/shard_map/ppermute | solution.py:35
  167.1 28.0 %collective-permute-start.9 = (f32[64,6,6,128]{3,0,2,1:T(8,128)S(1)}, f32[64,6,6,128]{3,0,2,1:T(8,128)S(1)}, u32[]{:S(2)}, u32[]{:S(2)}) collective-permute-start(f32[64,6,6,128]{3,0,2,1:T(8,128)S(1)} %copy.104), channel_id=1, source_target_pairs={{0,16},{16,32},{32,48},{1,17},{17,33},{33,49},{2,18},{18,34},{34,5... | collective-permute-start | bytes 3538952 | tf_op jit(solution)/shard_map/ppermute | solution.py:35
  208.0 17.8 %collective-permute-start.12 = (bf16[64,6,128]{2,0,1:T(8,128)(2,1)S(1)}, bf16[64,6,128]{2,0,1:T(8,128)(2,1)S(1)}, u32[]{:S(2)}, u32[]{:S(2)}) collective-permute-start(bf16[64,6,128]{2,0,1:T(8,128)(2,1)S(1)} %get-tuple-element.120), channel_id=1, source_target_pairs={{16,0},{32,16},{48,32},{17,1},{33,17},{49,33},{18,2},{34,18},{50,3... | collective-permute-start | bytes 294920 | tf_op jit(solution)/shard_map/ppermute | solution.py:24
  210.3 11.7 %copy-start.13 = (f32[64,6,6,128]{3,0,2,1:T(8,128)S(1)}, f32[64,6,6,128]{3,0,2,1:T(8,128)}, u32[]{:S(2)}) copy-start(f32[64,6,6,128]{3,0,2,1:T(8,128)} %copy-done.12) | copy-start | bytes 3538948
  210.5 13.4 %copy-start.15 = (f32[64,6,6,128]{3,0,2,1:T(8,128)S(1)}, f32[64,6,6,128]{3,0,2,1:T(8,128)}, u32[]{:S(2)}) copy-start(f32[64,6,6,128]{3,0,2,1:T(8,128)} %copy-done.14) | copy-start | bytes 3538948
  210.5 17.2 %collective-permute-start.13 = (bf16[64,6,128]{2,0,1:T(8,128)(2,1)S(1)}, bf16[64,6,128]{2,0,1:T(8,128)(2,1)S(1)}, u32[]{:S(2)}, u32[]{:S(2)}) collective-permute-start(bf16[64,6,128]{2,0,1:T(8,128)(2,1)S(1)} %get-tuple-element.119), channel_id=1, source_target_pairs={{0,16},{16,32},{32,48},{1,17},{17,33},{33,49},{2,18},{18,34},{34,5... | collective-permute-start | bytes 294920 | tf_op jit(solution)/shard_map/ppermute | solution.py:24
  215.9 18.3 %collective-permute-start.14 = (f32[64,6,128]{2,1,0:T(8,128)}, f32[64,6,128]{2,1,0:T(8,128)S(1)}, u32[]{:S(2)}, u32[]{:S(2)}) collective-permute-start(f32[64,6,128]{2,1,0:T(8,128)} %get-tuple-element.109), channel_id=1, source_target_pairs={{1,0},{2,1},{3,2},{4,3},{5,4},{6,5},{7,6},{8,7},{9,8},{10,9},{11,1... | collective-permute-start | bytes 589832 | tf_op jit(solution)/shard_map/ppermute | solution.py:24
  217.2 18.7 %collective-permute-start.15 = (f32[64,6,128]{2,1,0:T(8,128)}, f32[64,6,128]{2,1,0:T(8,128)S(1)}, u32[]{:S(2)}, u32[]{:S(2)}) collective-permute-start(f32[64,6,128]{2,1,0:T(8,128)} %get-tuple-element.108), channel_id=1, source_target_pairs={{0,1},{1,2},{2,3},{3,4},{4,5},{5,6},{6,7},{7,8},{8,9},{9,10},{10,1... | collective-permute-start | bytes 589832 | tf_op jit(solution)/shard_map/ppermute | solution.py:24
  227.7 9.8 %copy-start.2 = (f32[64,6,6,128]{3,1,0,2:T(8,128)S(1)}, f32[64,6,6,128]{3,1,0,2:T(8,128)}, u32[]{:S(2)}) copy-start(f32[64,6,6,128]{3,1,0,2:T(8,128)} %copy-done.1) | copy-start | bytes 3538948
  227.7 9.8 %copy-start.4 = (f32[64,6,6,128]{3,0,2,1:T(8,128)S(1)}, f32[64,6,6,128]{3,0,2,1:T(8,128)}, u32[]{:S(2)}) copy-start(f32[64,6,6,128]{3,0,2,1:T(8,128)} %param.23) | copy-start | bytes 3538948
  254.9 68.4 %copy-start.7 = (f32[64,6,6,128]{3,1,0,2:T(8,128)S(1)}, f32[64,6,6,128]{3,1,0,2:T(8,128)}, u32[]{:S(2)}) copy-start(f32[64,6,6,128]{3,1,0,2:T(8,128)} %get-tuple-element.105) | copy-start | bytes 3538948
  254.9 692.0 %all-reduce.4.cloned.1.call-start = ((), (), s32[]{:S(2)}) async-start(), calls=%async_computation.1 | async-start | bytes 131072 | tf_op jit(solution)/shard_map/psum | solution.py:173
  (7 other events, 12.4 us)
Sparse Core Ops, SparseCore 0:
  255.0 64.9 all-gather.1
  323.5 623.4 all-reduce.3
where the time goes:
time: 957 us; the launch traced here: 955 us
  waiting for transfers between devices  749 us (78%)
  local copies, waits for them, and re-layouts  71.6 us (7%)
  other arithmetic  58.9 us (6%)
  starting transfers between devices  48.6 us (5%)
  between operations  14.6 us (2%)
  matrix products  12.6 us (1%)
    psum x1, waiting for transfers between devices, local(): gram = lax.psum(partial_rows, ('sx', 'sy')) / cell_total  622 us
    all_gather x1, waiting for transfers between devices, local(): lax.all_gather(flat, 'band', axis=0, tiled=True)  65 us
    ppermute x4, waiting for transfers between devices, extended(): lax.ppermute(head, axis, [((i + 1) % count, i) for i in range(ends)])  58.8 us
    div x1, other arithmetic, local(): current = (apply_h(orbitals) - filter_center * orbitals) / filter_half  34.7 us
    ppermute x8, starting transfers between devices, from_behind(): return lax.ppermute(block, axis, route)  25.2 us
    concatenate x2, local copies, waits for them, and re-layouts, nonlocal_term(): jnp.concatenate([field.reshape(batch, inner, count_z), ext_x[:, 5], ext_x...  20.6 us
  transfers between devices with their start and end apart: 18, of which 8 were waited for; matrix products, arithmetic and copies ran while one was open for 5% of the time, Pallas kernels for 0%

commit v1 on v0

--- a/solution.py
+++ b/solution.py
@@ -170,7 +170,7 @@
         preferred_element_type=jnp.float32,
     )
     cell_total = flat.shape[1] * lax.axis_size("sx") * lax.axis_size("sy")
-    gram = lax.psum(partial_rows, ("sx", "sy")) / cell_total
+    gram = lax.psum(lax.psum(partial_rows, "sy"), "sx") / cell_total
     return (current, gram)
 
 

time: 957 us -> 532 us (0.56)
  waiting for transfers between devices: 749 us -> 323 us
    psum x1 -> x2, waiting for transfers between devices: 622 us -> 196 us  [local(): gram = lax.psum(lax.psum(partial_rows, 'sy'), 'sx') / cell_total]
  transfers between devices with their start and end apart: 18 -> 19, of which waited for: 8 -> 9; matrix products, arithmetic and copies ran while one was open for 5% -> 8% of each run, Pallas kernels for 0% -> 0%
where the time goes in v1:
time: 532 us; the launch traced here: 529 us
  waiting for transfers between devices  323 us (61%)
  local copies, waits for them, and re-layouts  71.6 us (13%)
  other arithmetic  58.9 us (11%)
  starting transfers between devices  48.6 us (9%)
  between operations  14.3 us (3%)
  matrix products  12.6 us (2%)
    psum x2, waiting for transfers between devices, local(): gram = lax.psum(lax.psum(partial_rows, 'sy'), 'sx') / cell_total  196 us
    all_gather x1, waiting for transfers between devices, local(): lax.all_gather(flat, 'band', axis=0, tiled=True)  65 us
    ppermute x4, waiting for transfers between devices, extended(): lax.ppermute(head, axis, [((i + 1) % count, i) for i in range(ends)])  58.8 us
    div x1, other arithmetic, local(): current = (apply_h(orbitals) - filter_center * orbitals) / filter_half  34.7 us
    ppermute x8, starting transfers between devices, from_behind(): return lax.ppermute(block, axis, route)  25.2 us
    concatenate x2, local copies, waits for them, and re-layouts, nonlocal_term(): jnp.concatenate([field.reshape(batch, inner, count_z), ext_x[:, 5], ext_x...  20.6 us
    ppermute x4, starting transfers between devices, extended(): lax.ppermute(tail, axis, [(i, (i + 1) % count) for i in range(ends)])  18.1 us
    convert_element_type x1, other arithmetic, local(): rounded = current.astype(jnp.bfloat16)  15.2 us
  transfers between devices with their start and end apart: 19, of which 9 were waited for; matrix products, arithmetic and copies ran while one was open for 8% of the time, Pallas kernels for 0%

profile of v1, /device:TPU:128, one launch (start us, length us, event | category | flops | bytes accessed | tf_op | source)
XLA Modules:
  0.0 529.1 jit_solution(18216215684204924326)
XLA Ops:
  8.6 4.6 collective-permute-start.1
  13.2 4.0 collective-permute-start.3
  18.5 3.1 copy.96
  21.8 15.3 %collective-permute-done = f32[64,6,6,128]{3,0,2,1:T(8,128)S(1)} collective-permute-done((f32[64,6,6,128]{3,0,2,1:T(8,128)}, f32[64,6,6,128]{3,0,2,1:T(8,128)S(1)}, u32[]{:S(2)}, u32[]{:S(2)}) %collective-permute-start) | collective-permute-done | bytes 1179680 | tf_op jit(solution)/shard_map/ppermute | solution.py:37
  41.1 2.0 copy_dynamic-update-slice_fusion.2
  43.1 2.5 copy_dynamic-update-slice_fusion
  45.6 25.1 %collective-permute-done.2 = f32[64,6,6,128]{3,0,2,1:T(8,128)} collective-permute-done((f32[64,6,6,128]{3,0,2,1:T(8,128)}, f32[64,6,6,128]{3,0,2,1:T(8,128)}, u32[]{:S(2)}, u32[]{:S(2)}) %collective-permute-start.2) | collective-permute-done | bytes 1179680 | tf_op jit(solution)/shard_map/ppermute | solution.py:37
  70.7 3.1 copy_dynamic-update-slice_fusion.3
  74.7 14.2 %concatenate.86 = f32[64,60,128]{2,1,0:T(8,128)} concatenate(f32[64,36,128]{2,1,0:T(8,128)} %copy.96, f32[64,6,128]{2,1,0:T(8,128)} %bitcast.115, f32[64,6,128]{2,1,0:T(8,128)S(1)} %bitcast.114, f32[64,6,128]{2,1,0:T(8,128)} %get-tuple-element.126, f32[64,6,128]{2,1,0:T(8,128)} %get-tuple-element.125), dimensions={1} | concatenate | bytes 3932160 | tf_op jit(solution)/shard_map/concatenate | solution.py:104
  88.9 2.5 convolution_bitcast_fusion.3
  98.2 4.7 collective-permute-start.5
  104.2 5.3 collective-permute-start.7
  109.4 1.9 copy.78
  111.4 1.8 copy.79
  115.3 6.1 %scatter-add.29 = f32[64,6,6,128]{3,1,0,2:T(8,128)} dynamic-update-slice(f32[64,6,6,128]{3,1,0,2:T(8,128)} %copy.102, f32[64,1,6,128]{3,1,0,2:T(1,128)S(1)} %add.432, s32[]{:T(128)} %constant.233.clone.1, s32[]{:T(128)} %constant.233.clone.1, s32[]{:T(128)} %constant.233.clone.1, s32[]{:T(128)} %constant.233.clone.1) | dynamic-update-slice | bytes 393220 | tf_op jit(solution)/shard_map/scatter-add | solution.py:130
  124.9 34.7 %broadcast_multiply_fusion = (f32[64,6,6,128]{3,1,0,2:T(8,128)S(1)}, f32[64,6,6,128]{3,1,0,2:T(8,128)}) fusion(f32[64,6,6,128]{3,1,0,2:T(8,128)} %get-tuple-element.116, f32[64,6,6,128]{3,1,0,2:T(8,128)} %fusion.135, f32[6,6,128]{2,0,1:T(8,128)S(1)} %copy.90, f32[64,6,6,128]{3,0,2,1:T(8,128)} %collective-permute-done.3, ...), kind=kLoop, calls=%fused_computation.225 | loop fusion | flops 21233664 | bytes 21252096 | tf_op jit(solution)/shard_map/div | solution.py:161
  162.5 4.6 collective-permute-start.11
  167.1 4.8 collective-permute-start.9
  172.7 15.8 %collective-permute-done.8 = f32[64,6,6,128]{3,0,2,1:T(8,128)S(1)} collective-permute-done((f32[64,6,6,128]{3,0,2,1:T(8,128)S(1)}, f32[64,6,6,128]{3,0,2,1:T(8,128)S(1)}, u32[]{:S(2)}, u32[]{:S(2)}) %collective-permute-start.8) | collective-permute-done | bytes 1179680 | tf_op jit(solution)/shard_map/ppermute | solution.py:37
  189.6 2.6 collective-permute-done.10
  196.3 6.5 %concatenate.91 = f32[64,60,128]{2,1,0:T(8,128)S(1)} concatenate(f32[64,36,128]{2,1,0:T(8,128)S(1)} %copy.122, f32[64,6,128]{2,1,0:T(8,128)} %bitcast.117, f32[64,6,128]{2,1,0:T(8,128)} %bitcast.116, f32[64,6,128]{2,1,0:T(8,128)} %slice_bitcast_fusion.1, f32[64,6,128]{2,1,0:T(8,128)} %slice_bitcast_fusion), dimensions={1} | concatenate | bytes 3932160 | tf_op jit(solution)/shard_map/concatenate | solution.py:104
  210.5 5.3 %collective-permute-start.13 = (bf16[64,6,128]{2,0,1:T(8,128)(2,1)S(1)}, bf16[64,6,128]{2,0,1:T(8,128)(2,1)S(1)}, u32[]{:S(2)}, u32[]{:S(2)}) collective-permute-start(bf16[64,6,128]{2,0,1:T(8,128)(2,1)S(1)} %get-tuple-element.119), channel_id=1, source_target_pairs={{0,16},{16,32},{32,48},{1,17},{17,33},{33,49},{2,18},{18,34},{34,5... | collective-permute-start | bytes 294920 | tf_op jit(solution)/shard_map/ppermute | solution.py:24
  217.2 4.8 collective-permute-start.15
  222.0 1.9 copy.105
  223.9 1.9 copy.107
  225.9 1.8 copy.128
  227.9 6.2 %scatter-add.35 = f32[64,6,6,128]{3,1,0,2:T(8,128)} dynamic-update-slice(f32[64,6,6,128]{3,1,0,2:T(8,128)} %copy.128, f32[64,1,6,128]{3,1,0,2:T(1,128)S(1)} %add.474, s32[]{:T(128)} %constant.233.clone.1, s32[]{:T(128)} %constant.233.clone.1, s32[]{:T(128)} %constant.233.clone.1, s32[]{:T(128)} %constant.233.clone.1) | dynamic-update-slice | bytes 393220 | tf_op jit(solution)/shard_map/scatter-add | solution.py:130
  237.5 15.2 %fusion.152 = (bf16[64,6,6,128]{3,1,0,2:T(8,128)(2,1)S(1)}, f32[64,6,6,128]{3,1,0,2:T(8,128)}) fusion(f32[64,6,6,128]{3,0,2,1:T(8,128)S(1)} %copy-done.4, f32[64,6,6,128]{3,1,0,2:T(8,128)} %get-tuple-element.107, f32[64,6,6,128]{3,1,0,2:T(8,128)} %fusion.133, f32[6,6,128]{2,0,1:T(8,128)S(1)} %copy.116, f32[64,6,6,128]{3,1,0,2:T(8,128)} %copy-done.5, ...), kind=kLoop, calls=%fused_computation.274 | loop fusion | flops 24772608 | bytes 11225088 | tf_op jit(solution)/shard_map/convert_element_type | solution.py:164
  255.0 65.0 %all-gather.2.cloned.1.call-done = bf16[256,4608]{1,0:T(8,128)(2,1)} async-done(((bf16[64,4608]{1,0:T(8,128)(2,1)}), bf16[256,4608]{1,0:T(8,128)(2,1)}) %all-gather.2.cloned.1.call-update) | async-done | bytes 2359312 | tf_op jit(solution)/shard_map/all_gather | solution.py:168
  320.0 3.3 fusion.160
  323.4 150.5 %all-reduce.5.cloned.1.call-done = f32[64,256]{1,0:T(8,128)} async-done(((f32[64,256]{1,0:T(8,128)}), f32[64,256]{1,0:T(8,128)}) %all-reduce.5.cloned.1.call-update) | async-done | bytes 65552 | tf_op jit(solution)/shard_map/psum | solution.py:173
  475.1 45.9 %all-reduce.7.cloned.1.call-done = f32[64,256]{1,0:T(8,128)} async-done(((f32[64,256]{1,0:T(8,128)}), f32[64,256]{1,0:T(8,128)}) %all-reduce.7.cloned.1.call-update) | async-done | bytes 65552 | tf_op jit(solution)/shard_map/psum | solution.py:173
  (125 shorter events, 47.7 us)
Async XLA Ops:
  7.2 84.3 %copy-start = (f32[4,4,5,128]{3,1,2,0:T(4,128)S(1)}, f32[4,4,5,128]{3,1,2,0:T(4,128)}, u32[]{:S(2)}) copy-start(f32[4,4,5,128]{3,1,2,0:T(4,128)} %param.25) | copy-start | bytes 122884
  7.2 14.5 %copy-start.19 = (s32[5]{0:T(128)S(1)}, s32[5]{0:T(128)}, u32[]{:S(2)}) copy-start(s32[5]{0:T(128)} %constant.246.clone) | copy-start | bytes 64
  7.2 14.5 %copy-start.20 = (s32[5]{0:T(128)S(1)}, s32[5]{0:T(128)}, u32[]{:S(2)}) copy-start(s32[5]{0:T(128)} %constant.247.clone) | copy-start | bytes 64
  7.2 14.4 %copy-start.18 = (s32[4,2]{0,1:T(2,128)S(1)}, s32[4,2]{0,1:T(2,128)}, u32[]{:S(2)}) copy-start(s32[4,2]{0,1:T(2,128)} %param.27) | copy-start | bytes 100
  7.2 14.6 %copy-start.16 = (f32[6,6,128]{2,1,0:T(8,128)S(1)}, f32[6,6,128]{2,1,0:T(8,128)}, u32[]{:S(2)}) copy-start(f32[6,6,128]{2,1,0:T(8,128)} %param.24) | copy-start | bytes 55300
  7.2 312.8 %all-gather.2.cloned.1.call-start = ((), (), s32[]{:S(2)}) async-start(), calls=%async_computation | async-start | bytes 2949120 | tf_op jit(solution)/shard_map/all_gather | solution.py:168
  7.3 29.8 %collective-permute-start = (f32[64,6,6,128]{3,0,2,1:T(8,128)}, f32[64,6,6,128]{3,0,2,1:T(8,128)S(1)}, u32[]{:S(2)}, u32[]{:S(2)}) collective-permute-start(f32[64,6,6,128]{3,0,2,1:T(8,128)} %param.23), channel_id=1, source_target_pairs={{16,0},{32,16},{48,32},{17,1},{33,17},{49,33},{18,2},{34,18},{50,3... | collective-permute-start | bytes 3538952 | tf_op jit(solution)/shard_map/ppermute | solution.py:37
  8.6 29.8 %collective-permute-start.1 = (f32[64,6,6,128]{3,0,2,1:T(8,128)}, f32[64,6,6,128]{3,0,2,1:T(8,128)S(1)}, u32[]{:S(2)}, u32[]{:S(2)}) collective-permute-start(f32[64,6,6,128]{3,0,2,1:T(8,128)} %param.23), channel_id=1, source_target_pairs={{0,16},{16,32},{32,48},{1,17},{17,33},{33,49},{2,18},{18,34},{34,5... | collective-permute-start | bytes 3538952 | tf_op jit(solution)/shard_map/ppermute | solution.py:35
  13.2 27.9 %collective-permute-start.3 = (f32[64,6,6,128]{3,0,2,1:T(8,128)}, f32[64,6,6,128]{3,0,2,1:T(8,128)}, u32[]{:S(2)}, u32[]{:S(2)}) collective-permute-start(f32[64,6,6,128]{3,0,2,1:T(8,128)} %param.23), channel_id=1, source_target_pairs={{0,1},{1,2},{2,3},{3,4},{4,5},{5,6},{6,7},{7,8},{8,9},{9,10},{10,1... | collective-permute-start | bytes 3538952 | tf_op jit(solution)/shard_map/ppermute | solution.py:35
  17.2 53.5 %collective-permute-start.2 = (f32[64,6,6,128]{3,0,2,1:T(8,128)}, f32[64,6,6,128]{3,0,2,1:T(8,128)}, u32[]{:S(2)}, u32[]{:S(2)}) collective-permute-start(f32[64,6,6,128]{3,0,2,1:T(8,128)} %param.23), channel_id=1, source_target_pairs={{1,0},{2,1},{3,2},{4,3},{5,4},{6,5},{7,6},{8,7},{9,8},{10,9},{11,1... | collective-permute-start | bytes 3538952 | tf_op jit(solution)/shard_map/ppermute | solution.py:37
  95.7 17.5 %collective-permute-start.4 = (bf16[64,6,128]{2,0,1:T(8,128)(2,1)S(1)}, bf16[64,6,128]{2,0,1:T(8,128)(2,1)S(1)}, u32[]{:S(2)}, u32[]{:S(2)}) collective-permute-start(bf16[64,6,128]{2,0,1:T(8,128)(2,1)S(1)} %get-tuple-element.122), channel_id=1, source_target_pairs={{16,0},{32,16},{48,32},{17,1},{33,17},{49,33},{18,2},{34,18},{50,3... | collective-permute-start | bytes 294920 | tf_op jit(solution)/shard_map/ppermute | solution.py:24
  97.9 11.5 %copy-start.9 = (f32[64,6,6,128]{3,0,2,1:T(8,128)S(1)}, f32[64,6,6,128]{3,0,2,1:T(8,128)}, u32[]{:S(2)}) copy-start(f32[64,6,6,128]{3,0,2,1:T(8,128)} %copy-done.8) | copy-start | bytes 3538948
  98.2 13.2 %copy-start.11 = (f32[64,6,6,128]{3,0,2,1:T(8,128)S(1)}, f32[64,6,6,128]{3,0,2,1:T(8,128)}, u32[]{:S(2)}) copy-start(f32[64,6,6,128]{3,0,2,1:T(8,128)} %copy-done.10) | copy-start | bytes 3538948
  98.2 16.9 %collective-permute-start.5 = (bf16[64,6,128]{2,0,1:T(8,128)(2,1)S(1)}, bf16[64,6,128]{2,0,1:T(8,128)(2,1)S(1)}, u32[]{:S(2)}, u32[]{:S(2)}) collective-permute-start(bf16[64,6,128]{2,0,1:T(8,128)(2,1)S(1)} %get-tuple-element.121), channel_id=1, source_target_pairs={{0,16},{16,32},{32,48},{1,17},{17,33},{33,49},{2,18},{18,34},{34,5... | collective-permute-start | bytes 294920 | tf_op jit(solution)/shard_map/ppermute | solution.py:24
  102.9 18.5 %collective-permute-start.6 = (f32[64,6,128]{2,1,0:T(8,128)}, f32[64,6,128]{2,1,0:T(8,128)}, u32[]{:S(2)}, u32[]{:S(2)}) collective-permute-start(f32[64,6,128]{2,1,0:T(8,128)} %get-tuple-element.111), channel_id=1, source_target_pairs={{1,0},{2,1},{3,2},{4,3},{5,4},{6,5},{7,6},{8,7},{9,8},{10,9},{11,1... | collective-permute-start | bytes 589832 | tf_op jit(solution)/shard_map/ppermute | solution.py:24
  104.2 19.0 %collective-permute-start.7 = (f32[64,6,128]{2,1,0:T(8,128)}, f32[64,6,128]{2,1,0:T(8,128)}, u32[]{:S(2)}, u32[]{:S(2)}) collective-permute-start(f32[64,6,128]{2,1,0:T(8,128)} %get-tuple-element.110), channel_id=1, source_target_pairs={{0,1},{1,2},{2,3},{3,4},{4,5},{5,6},{6,7},{7,8},{8,9},{9,10},{10,1... | collective-permute-start | bytes 589832 | tf_op jit(solution)/shard_map/ppermute | solution.py:24
  159.6 13.1 %copy-start.1 = (f32[64,6,6,128]{3,1,0,2:T(8,128)}, f32[64,6,6,128]{3,1,0,2:T(8,128)S(1)}, u32[]{:S(2)}) copy-start(f32[64,6,6,128]{3,1,0,2:T(8,128)S(1)} %get-tuple-element.106) | copy-start | bytes 3538948
  159.9 28.7 %collective-permute-start.8 = (f32[64,6,6,128]{3,0,2,1:T(8,128)S(1)}, f32[64,6,6,128]{3,0,2,1:T(8,128)S(1)}, u32[]{:S(2)}, u32[]{:S(2)}) collective-permute-start(f32[64,6,6,128]{3,0,2,1:T(8,128)S(1)} %copy.104), channel_id=1, source_target_pairs={{16,0},{32,16},{48,32},{17,1},{33,17},{49,33},{18,2},{34,18},{50,3... | collective-permute-start | bytes 3538952 | tf_op jit(solution)/shard_map/ppermute | solution.py:37
  161.2 31.0 %collective-permute-start.10 = (f32[64,6,6,128]{3,0,2,1:T(8,128)S(1)}, f32[64,6,6,128]{3,0,2,1:T(8,128)S(1)}, u32[]{:S(2)}, u32[]{:S(2)}) collective-permute-start(f32[64,6,6,128]{3,0,2,1:T(8,128)S(1)} %copy.104), channel_id=1, source_target_pairs={{1,0},{2,1},{3,2},{4,3},{5,4},{6,5},{7,6},{8,7},{9,8},{10,9},{11,1... | collective-permute-start | bytes 3538952 | tf_op jit(solution)/shard_map/ppermute | solution.py:37
  162.5 30.4 %collective-permute-start.11 = (f32[64,6,6,128]{3,0,2,1:T(8,128)S(1)}, f32[64,6,6,128]{3,0,2,1:T(8,128)S(1)}, u32[]{:S(2)}, u32[]{:S(2)}) collective-permute-start(f32[64,6,6,128]{3,0,2,1:T(8,128)S(1)} %copy.104), channel_id=1, source_target_pairs={{0,1},{1,2},{2,3},{3,4},{4,5},{5,6},{6,7},{7,8},{8,9},{9,10},{10,1... | collective-permute-start | bytes 3538952 | tf_op jit(solution)/shard_map/ppermute | solution.py:35
  167.1 28.0 %collective-permute-start.9 = (f32[64,6,6,128]{3,0,2,1:T(8,128)S(1)}, f32[64,6,6,128]{3,0,2,1:T(8,128)S(1)}, u32[]{:S(2)}, u32[]{:S(2)}) collective-permute-start(f32[64,6,6,128]{3,0,2,1:T(8,128)S(1)} %copy.104), channel_id=1, source_target_pairs={{0,16},{16,32},{32,48},{1,17},{17,33},{33,49},{2,18},{18,34},{34,5... | collective-permute-start | bytes 3538952 | tf_op jit(solution)/shard_map/ppermute | solution.py:35
  208.0 17.8 %collective-permute-start.12 = (bf16[64,6,128]{2,0,1:T(8,128)(2,1)S(1)}, bf16[64,6,128]{2,0,1:T(8,128)(2,1)S(1)}, u32[]{:S(2)}, u32[]{:S(2)}) collective-permute-start(bf16[64,6,128]{2,0,1:T(8,128)(2,1)S(1)} %get-tuple-element.120), channel_id=1, source_target_pairs={{16,0},{32,16},{48,32},{17,1},{33,17},{49,33},{18,2},{34,18},{50,3... | collective-permute-start | bytes 294920 | tf_op jit(solution)/shard_map/ppermute | solution.py:24
  210.3 11.7 %copy-start.13 = (f32[64,6,6,128]{3,0,2,1:T(8,128)S(1)}, f32[64,6,6,128]{3,0,2,1:T(8,128)}, u32[]{:S(2)}) copy-start(f32[64,6,6,128]{3,0,2,1:T(8,128)} %copy-done.12) | copy-start | bytes 3538948
  210.5 13.4 %copy-start.15 = (f32[64,6,6,128]{3,0,2,1:T(8,128)S(1)}, f32[64,6,6,128]{3,0,2,1:T(8,128)}, u32[]{:S(2)}) copy-start(f32[64,6,6,128]{3,0,2,1:T(8,128)} %copy-done.14) | copy-start | bytes 3538948
  210.5 17.2 %collective-permute-start.13 = (bf16[64,6,128]{2,0,1:T(8,128)(2,1)S(1)}, bf16[64,6,128]{2,0,1:T(8,128)(2,1)S(1)}, u32[]{:S(2)}, u32[]{:S(2)}) collective-permute-start(bf16[64,6,128]{2,0,1:T(8,128)(2,1)S(1)} %get-tuple-element.119), channel_id=1, source_target_pairs={{0,16},{16,32},{32,48},{1,17},{17,33},{33,49},{2,18},{18,34},{34,5... | collective-permute-start | bytes 294920 | tf_op jit(solution)/shard_map/ppermute | solution.py:24
  215.9 18.3 %collective-permute-start.14 = (f32[64,6,128]{2,1,0:T(8,128)}, f32[64,6,128]{2,1,0:T(8,128)S(1)}, u32[]{:S(2)}, u32[]{:S(2)}) collective-permute-start(f32[64,6,128]{2,1,0:T(8,128)} %get-tuple-element.109), channel_id=1, source_target_pairs={{1,0},{2,1},{3,2},{4,3},{5,4},{6,5},{7,6},{8,7},{9,8},{10,9},{11,1... | collective-permute-start | bytes 589832 | tf_op jit(solution)/shard_map/ppermute | solution.py:24
  217.2 18.7 %collective-permute-start.15 = (f32[64,6,128]{2,1,0:T(8,128)}, f32[64,6,128]{2,1,0:T(8,128)S(1)}, u32[]{:S(2)}, u32[]{:S(2)}) collective-permute-start(f32[64,6,128]{2,1,0:T(8,128)} %get-tuple-element.108), channel_id=1, source_target_pairs={{0,1},{1,2},{2,3},{3,4},{4,5},{5,6},{6,7},{7,8},{8,9},{9,10},{10,1... | collective-permute-start | bytes 589832 | tf_op jit(solution)/shard_map/ppermute | solution.py:24
  227.7 9.8 %copy-start.2 = (f32[64,6,6,128]{3,1,0,2:T(8,128)S(1)}, f32[64,6,6,128]{3,1,0,2:T(8,128)}, u32[]{:S(2)}) copy-start(f32[64,6,6,128]{3,1,0,2:T(8,128)} %copy-done.1) | copy-start | bytes 3538948
  227.7 9.8 %copy-start.4 = (f32[64,6,6,128]{3,0,2,1:T(8,128)S(1)}, f32[64,6,6,128]{3,0,2,1:T(8,128)}, u32[]{:S(2)}) copy-start(f32[64,6,6,128]{3,0,2,1:T(8,128)} %param.23) | copy-start | bytes 3538948
  254.9 219.0 %copy-start.7 = (f32[64,6,6,128]{3,1,0,2:T(8,128)S(1)}, f32[64,6,6,128]{3,1,0,2:T(8,128)}, u32[]{:S(2)}) copy-start(f32[64,6,6,128]{3,1,0,2:T(8,128)} %get-tuple-element.105) | copy-start | bytes 3538948
  254.9 218.9 %all-reduce.5.cloned.1.call-start = ((), (), s32[]{:S(2)}) async-start(), calls=%async_computation.1 | async-start | bytes 131072 | tf_op jit(solution)/shard_map/psum | solution.py:173
  323.4 197.7 %all-reduce.7.cloned.1.call-start = ((), (), s32[]{:S(2)}) async-start(), calls=%async_computation.2 | async-start | bytes 131072 | tf_op jit(solution)/shard_map/psum | solution.py:173
  (8 other events, 16.0 us)
Sparse Core Ops, SparseCore 0:
  255.0 64.9 all-gather.1
  323.5 150.3 all-reduce.4
  476.3 44.7 all-reduce.6
